TPU v7x, 256 devices: a whole 4x4x8 slice. The times are simulated.
256 devices in a mesh: row: 8 (over z_hi, y), col: 32 (over x, z_lo, core).
Axes of the slice: x: 4, y: 4, z: 8 (z_hi: 2, z_lo: 4; z = z_hi * 4 + z_lo), core: 2. Of those that a mesh axis runs over, the one named last changes fastest.
Arguments:
- active_matrix: float32 [16384, 16384], P('row', 'col'), may hold values from -6 to 6
- schur_rows: float32 [2048, 16384], P('row', 'col'), may hold values from -6 to 6
- accum_first: float32 [32, 512, 512], P('row', 'col'), may hold values from -1 to 1, as said below
- accum_second: float32 [32, 512, 512], P('row', 'col'), may hold values from -1 to 1, as said below
Outputs:
- matrix_out: float32 [16384, 16384], P('row', 'col')
- schur_out: float32 [2048, 16384], P('row', 'col')
Inputs may be any that keep to these rules, and one draw needn't show every extreme that they name: `accum_first`: each of the 32 blocks of order 512 is an orthogonal matrix. `accum_second`: each of the 32 blocks of order 512 is an orthogonal matrix.
All inputs are finite; a program needn't handle non-finite values.
Results may differ from a plain program's by a relative error of at most 0.000098.
Values sent between devices are 32-bit elements; how exact they have to be, the bound alone decides.
A program may use at most 128 MiB of HBM per device.

v0:
```python
import jax
import jax.numpy as jnp
from jax import lax
from jax.sharding import PartitionSpec as P


def spread(array, axis, root):
    mine = lax.axis_index(axis) == root
    return lax.psum(jnp.where(mine, array, jnp.zeros_like(array)), axis)


def passed_along(block, axis, distance):
    devices = range(lax.axis_size(axis))
    route = [((i - distance) % len(devices), i) for i in devices]
    return lax.ppermute(block, axis, route)


def padded(block, sides, width):
    for axis, dim in sides:
        count = lax.axis_size(axis)
        forward = [(i, i + 1) for i in range(count - 1)]
        forward.append((count - 1, 0))
        backward = [(target, source) for source, target in forward]
        low = lax.ppermute(
            lax.slice_in_dim(block, block.shape[dim] - width, None, axis=dim), axis, forward
        )
        high = lax.ppermute(lax.slice_in_dim(block, 0, width, axis=dim), axis, backward)
        block = jnp.concatenate([low, block, high], axis=dim)
    return block


def exact_dot(left, right):
    return jnp.dot(left, right, precision=lax.Precision.HIGHEST, preferred_element_type=jnp.float32)


def aligned_right(matrix, blocks):
    rows, cols = matrix.shape
    count, width = (blocks.shape[0], blocks.shape[1])
    shaped = matrix.reshape(rows, count, width)
    out = jnp.einsum("nki,kij->nkj", shaped, blocks, precision=lax.Precision.HIGHEST)
    return out.reshape(rows, cols)


def straddle_right(extended, blocks, half):
    width = blocks.shape[1]
    count = blocks.shape[0] - 1
    head = exact_dot(extended[:, :width], blocks[0][:, half:])
    tail = exact_dot(extended[:, count * width :], blocks[count][:, :half])
    pieces = [head]
    pieces.append(tail)
    return jnp.concatenate(pieces, axis=1)


def straddle_left(blocks, extended, half):
    cols = extended.shape[1]
    width = blocks.shape[1]
    count = blocks.shape[0] - 1
    head = jnp.einsum(
        "ij,in->jn", blocks[0][:, half:], extended[:width], precision=lax.Precision.HIGHEST
    )
    tail = jnp.einsum(
        "ij,in->jn",
        blocks[count][:, :half],
        extended[count * width :],
        precision=lax.Precision.HIGHEST,
    )
    pieces = [head]
    inner = extended[width : count * width].reshape(count - 1, width, cols)
    middle = jnp.einsum("kij,kin->kjn", blocks[1:count], inner, precision=lax.Precision.HIGHEST)
    pieces.append(middle.reshape((count - 1) * width, cols))
    pieces.append(tail)
    return jnp.concatenate(pieces, axis=0)


def per_device(active_matrix, schur_rows, accum_first, accum_second):
    width = accum_first.shape[2]
    half = width // 2
    row_tile, col_tile = active_matrix.shape
    per_row = row_tile // width
    per_col = col_tile // width
    col_index = lax.axis_index("col")
    owner_row = col_index * per_col // per_row
    owner_offset = col_index * per_col % per_row
    first_full = lax.all_gather(accum_first, "col", axis=1, tiled=True)
    shaped = active_matrix.reshape(per_row, width, col_tile)
    turned_rows = jnp.einsum(
        "kij,kin->kjn", first_full, shaped, precision=lax.Precision.HIGHEST
    ).reshape(row_tile, col_tile)
    chosen = lax.dynamic_slice_in_dim(first_full, owner_offset, per_col, 0)
    first_cols = spread(chosen, "row", owner_row)
    stacked = jnp.concatenate([turned_rows, schur_rows], axis=0)
    turned = aligned_right(stacked, first_cols)
    second_full = lax.all_gather(accum_second, "col", axis=1, tiled=True)
    chosen_second = lax.dynamic_slice_in_dim(second_full, owner_offset, per_col, 0)
    second_cols = spread(chosen_second, "row", owner_row)
    next_col = passed_along(second_cols, "col", -1)
    col_blocks = jnp.concatenate([second_cols, next_col], axis=0)
    next_row = passed_along(second_full[0:1], "row", -1)
    row_blocks = jnp.concatenate([second_full, next_row], axis=0)
    extended = padded(turned, (("col", 1),), half)
    moved = straddle_right(extended, col_blocks, half)
    matrix_part = moved[:row_tile]
    schur_out = moved[row_tile:]
    extended_rows = padded(matrix_part, (("row", 0),), half)
    matrix_out = straddle_left(row_blocks, extended_rows, half)
    return (matrix_out, schur_out)


def solution(mesh):
    in_specs = (P("row", "col"), P("row", "col"), P("row", "col", None), P("row", "col", None))
    out_specs = (P("row", "col"), P("row", "col"))
    return jax.shard_map(
        per_device, mesh=mesh, in_specs=in_specs, out_specs=out_specs, check_vma=False
    )
```

profile of v0, /device:TPU:194, one launch (start us, length us, event | category | flops | bytes accessed | tf_op | source)
XLA Modules:
  0.0 484.2 jit_solution(11832636954454555958)
XLA Ops:
  7.2 0.0 all-gather.5.cloned.1.call-start
  7.2 0.7 all-gather.5.cloned.1.call-update
  7.9 0.0 all-gather.3.cloned.1.call-start
  7.9 0.7 all-gather.3.cloned.1.call-update
  8.6 0.0 all-reduce.3.cloned.1.call-start
  8.7 63.8 %all-gather.5.cloned.1.call-done = f32[4,512,512]{2,1,0:T(8,128)} async-done(((f32[4,16,512]{2,1,0:T(8,128)}), f32[4,512,512]{2,1,0:T(8,128)}) %all-gather.5.cloned.1.call-update) | async-done | bytes 4194320 | tf_op jit(solution)/shard_map/all_gather | solution.py:93
  72.5 3.4 slice_bitcast_fusion
  75.9 60.3 %all-gather.3.cloned.1.call-done = f32[4,512,512]{2,1,0:T(8,128)} async-done(((f32[4,16,512]{2,1,0:T(8,128)}), f32[4,512,512]{2,1,0:T(8,128)}) %all-gather.3.cloned.1.call-update) | async-done | bytes 4194320 | tf_op jit(solution)/shard_map/all_gather | solution.py:84
  136.2 2.3 select_bitcast_fusion
  138.5 0.0 all-reduce.3.cloned.1.call-update
  138.5 0.0 copy-start.2
  138.5 11.9 %fusion.24 = f32[4,512,512]{2,1,0:T(8,128)} fusion(f32[4,512,512]{2,1,0:T(8,128)} %all-gather.3.cloned.1.call-done, f32[4,512,512]{2,1,0:T(8,128)} %bitcast.30), kind=kOutput, calls=%fused_computation.43 | convolution fusion | flops 6442450944 | bytes 12582912 | tf_op jit(solution)/shard_map/kij,kin->kjn/dot_general | solution.py:86
  150.4 121.9 %all-reduce.3.cloned.1.call-done = (f32[512,512]{1,0:T(8,128)}, f32[1,512,512]{2,1,0:T(8,128)}) async-done(((f32[512,512]{1,0:T(8,128)}, f32[1,512,512]{2,1,0:T(8,128)}), (f32[512,512]{1,0:T(8,128)}, f32[1,512,512]{2,1,0:T(8,128)})) %all-reduce.3.cloned.1.call-update) | async-done | bytes 2097168 | tf_op jit(solution)/shard_map/psum | solution.py:9
  272.3 29.2 %convolution_bitcast_fusion = f32[2304,512]{0,1:T(8,128)S(1)} fusion(f32[512,512]{1,0:T(8,128)} %get-tuple-element.6, f32[256,512]{1,0:T(8,128)S(1)} %copy-done.2, f32[2048,512]{1,0:T(8,128)} %bitcast.27), kind=kOutput, calls=%fused_computation.6 | convolution fusion | flops 7248936960 | bytes 10485760 | tf_op jit(solution)/shard_map/nki,kij->nkj/dot_general | solution.py:40
  301.5 0.3 fusion.23
  301.8 0.1 collective-permute-start
  301.9 1.7 collective-permute-start.1
  303.7 0.0 collective-permute-start.2
  303.7 0.9 collective-permute-start.5
  304.6 123.9 %collective-permute-done = f32[2304,256]{0,1:T(8,128)S(1)} collective-permute-done((f32[2304,256]{0,1:T(8,128)S(1)}, f32[2304,256]{0,1:T(8,128)S(1)}, u32[]{:S(2)}, u32[]{:S(2)}) %collective-permute-start) | collective-permute-done | bytes 2359328 | tf_op jit(solution)/shard_map/ppermute | solution.py:24
  428.5 4.3 fusion.2
  432.8 4.5 fusion
  437.3 2.4 fusion.8
  439.7 1.2 pad_maximum_fusion.9
  440.9 3.6 copy.9
  444.5 8.0 %collective-permute-start.4 = (f32[256,512]{0,1:T(8,128)}, f32[256,512]{0,1:T(8,128)}, u32[]{:S(2)}, u32[]{:S(2)}) collective-permute-start(f32[256,512]{0,1:T(8,128)} %get-tuple-element.10), channel_id=1, source_target_pairs={{32,0},{64,32},{96,64},{128,96},{160,128},{192,160},{224,192},{0,2... | collective-permute-start | bytes 1572872 | tf_op jit(solution)/shard_map/ppermute | solution.py:27
  452.5 13.7 %fusion.9 = f32[3,512,512]{1,2,0:T(8,128)} fusion(f32[3,512,512]{2,1,0:T(8,128)} %bitcast.28, f32[4,512,512]{2,1,0:T(8,128)} %all-gather.5.cloned.1.call-done), kind=kOutput, calls=%fused_computation.19 | convolution fusion | flops 4831838208 | bytes 9437184 | tf_op jit(solution)/shard_map/kij,kin->kjn/dot_general | solution.py:69
  466.2 2.0 copy.11
  468.2 2.0 fusion.7
  470.3 2.2 convolution_bitcast_fusion.2
  472.5 2.5 convolution_bitcast_fusion.1
  475.0 2.5 pad_maximum_fusion.4
  (13 shorter events, 0.0 us)
Async XLA Ops:
  7.2 65.3 %all-gather.5.cloned.1.call-start = ((), (), s32[]{:S(2)}) async-start(), calls=%async_computation.1 | async-start | bytes 4325376 | tf_op jit(solution)/shard_map/all_gather | solution.py:93
  7.9 128.3 %all-gather.3.cloned.1.call-start = ((), (), s32[]{:S(2)}) async-start(), calls=%async_computation | async-start | bytes 4325376 | tf_op jit(solution)/shard_map/all_gather | solution.py:84
  8.6 263.7 %all-reduce.3.cloned.1.call-start = ((), (), s32[]{:S(2)}) async-start(), calls=%async_computation.2 | async-start | bytes 4194304 | tf_op jit(solution)/shard_map/psum | solution.py:9
  138.5 133.8 %copy-start.2 = (f32[256,512]{1,0:T(8,128)S(1)}, f32[256,512]{1,0:T(8,128)}, u32[]{:S(2)}) copy-start(f32[256,512]{1,0:T(8,128)} %param.5) | copy-start | bytes 1572868
  301.5 2.2 copy-start.3
  301.8 126.7 %collective-permute-start = (f32[2304,256]{0,1:T(8,128)S(1)}, f32[2304,256]{0,1:T(8,128)S(1)}, u32[]{:S(2)}, u32[]{:S(2)}) collective-permute-start(f32[2304,256]{0,1:T(8,128)S(1)} %get-tuple-element.12), channel_id=1, source_target_pairs={{0,1},{1,2},{2,3},{3,4},{4,5},{5,6},{6,7},{7,8},{8,9},{9,10},{10,1... | collective-permute-start | bytes 7077896 | tf_op jit(solution)/shard_map/ppermute | solution.py:24
  301.9 130.9 %collective-permute-start.1 = (f32[2304,256]{0,1:T(8,128)S(1)}, f32[2304,256]{0,1:T(8,128)S(1)}, u32[]{:S(2)}, u32[]{:S(2)}) collective-permute-start(f32[2304,256]{0,1:T(8,128)S(1)} %get-tuple-element.11), channel_id=1, source_target_pairs={{1,0},{2,1},{3,2},{4,3},{5,4},{6,5},{7,6},{8,7},{9,8},{10,9},{11,1... | collective-permute-start | bytes 7077896 | tf_op jit(solution)/shard_map/ppermute | solution.py:27
  303.7 129.1 %collective-permute-start.2 = (f32[1,512,512]{2,1,0:T(8,128)S(1)}, f32[1,512,512]{2,1,0:T(8,128)S(1)}, u32[]{:S(2)}, u32[]{:S(2)}) collective-permute-start(f32[1,512,512]{2,1,0:T(8,128)S(1)} %copy-done.3), channel_id=1, source_target_pairs={{1,0},{2,1},{3,2},{4,3},{5,4},{6,5},{7,6},{8,7},{9,8},{10,9},{11,1... | collective-permute-start | bytes 3145736 | tf_op jit(solution)/shard_map/ppermute | solution.py:15
  303.7 168.8 %collective-permute-start.5 = (f32[1,512,512]{2,1,0:T(8,128)}, f32[1,512,512]{2,1,0:T(8,128)}, u32[]{:S(2)}, u32[]{:S(2)}) collective-permute-start(f32[1,512,512]{2,1,0:T(8,128)} %get-tuple-element.14), channel_id=1, source_target_pairs={{32,0},{64,32},{96,64},{128,96},{160,128},{192,160},{224,192},{0,2... | collective-permute-start | bytes 3145736 | tf_op jit(solution)/shard_map/ppermute | solution.py:15
  437.3 3.6 copy-start
  440.9 29.4 %collective-permute-start.3 = (f32[256,512]{0,1:T(8,128)}, f32[256,512]{0,1:T(8,128)}, u32[]{:S(2)}, u32[]{:S(2)}) collective-permute-start(f32[256,512]{0,1:T(8,128)} %get-tuple-element.9), channel_id=1, source_target_pairs={{0,32},{32,64},{64,96},{96,128},{128,160},{160,192},{192,224},{224... | collective-permute-start | bytes 1572872 | tf_op jit(solution)/shard_map/ppermute | solution.py:24
  444.5 28.0 %collective-permute-start.4 = (f32[256,512]{0,1:T(8,128)}, f32[256,512]{0,1:T(8,128)}, u32[]{:S(2)}, u32[]{:S(2)}) collective-permute-start(f32[256,512]{0,1:T(8,128)} %get-tuple-element.10), channel_id=1, source_target_pairs={{32,0},{64,32},{96,64},{128,96},{160,128},{192,160},{224,192},{0,2... | collective-permute-start | bytes 1572872 | tf_op jit(solution)/shard_map/ppermute | solution.py:27
  472.5 2.5 copy-start.1
Sparse Core Ops, SparseCore 0:
  9.9 62.5 all-gather.4
  74.3 61.8 all-gather.2
  138.9 133.3 all-reduce.2
where the time goes:
time: 488 us; the launch traced here: 484 us
  waiting for transfers between devices  371 us (76%)
  matrix products  68.1 us (14%)
  between operations  14.2 us (3%)
  other arithmetic  13.8 us (3%)
  starting transfers between devices  10.9 us (2%)
  local copies, waits for them, and re-layouts  5.94 us (1%)
    ppermute x2, waiting for transfers between devices, padded(): lax.ppermute(lax.slice_in_dim(block, block.shape[dim] - width, None, axis...  124 us
    psum x1, waiting for transfers between devices, spread(): return lax.psum(jnp.where(mine, array, jnp.zeros_like(array)), axis)  122 us
    all_gather x1, waiting for transfers between devices, per_device(): second_full = lax.all_gather(accum_second, 'col', axis=1, tiled=True)  63.8 us
    all_gather x1, waiting for transfers between devices, per_device(): first_full = lax.all_gather(accum_first, 'col', axis=1, tiled=True)  60.3 us
    dot_general x1, matrix products, aligned_right(): jnp.einsum('nki,kij->nkj', shaped, blocks, precision=lax.Precision.HIGHEST)  29.2 us
    dot_general x1, matrix products, straddle_left(): jnp.einsum('kij,kin->kjn', blocks[1:count], inner, precision=lax.Precisio...  13.7 us
    dot_general x1, matrix products, per_device(): jnp.einsum('kij,kin->kjn', first_full, shaped, precision=lax.Precision.HI...  11.9 us
    ppermute x2, starting transfers between devices, padded(): lax.ppermute(lax.slice_in_dim(block, 0, width, axis=dim), axis, backward)  9.77 us
  transfers between devices with their start and end apart: 9, of which 4 were waited for; matrix products, arithmetic and copies ran while one was open for 11% of the time, Pallas kernels for 0%

commit v1 on v0

v1 whole, which is shorter than its diff:
```python
import jax
import jax.numpy as jnp
from jax import lax
from jax.experimental import pallas as pl
from jax.experimental.pallas import tpu as pltpu
from jax.sharding import PartitionSpec as P

MESH = pl.DeviceIdType.MESH
F32 = jnp.float32
BF16 = jnp.bfloat16

W = 512
HALF = 256
ROWS = 2048
ZR = 256
BLOCKS = (ROWS + ZR) // 256


def split(a):
    high = a.astype(BF16)
    low = (a - high.astype(F32)).astype(BF16)
    return high, low


def product(a, b, dims):
    (a_high, a_low), (b_high, b_low) = a, b

    def dot(left, right):
        return lax.dot_general(left, right, (dims, ((), ())), preferred_element_type=F32)

    return (dot(a_low, b_high) + dot(a_high, b_low)) + dot(a_high, b_high)


def plain(a, b):
    return product(a, b, ((1,), (0,)))


def turned(a, b):
    return product(a, b, ((0,), (0,)))


def remote(src, dst, send, recv, device):
    return pltpu.make_async_remote_copy(
        src_ref=src, dst_ref=dst, send_sem=send, recv_sem=recv, device_id=device, device_id_type=MESH
    )


def at(start, size):
    return pl.ds(pl.multiple_of(start, size), size)


def block_of(position):
    return jnp.where(
        position < 2, position, jnp.where(position < 4, position + 4, jnp.where(position < 8, position - 2, 8))
    )


def window_of(position):
    return jnp.where(position == 0, 0, jnp.where(position == 1, 3, position - 1))


def kernel(
    h_ref, z_ref, u_ref, v_ref, ho_ref, zo_ref,
    tile, piece, gathered, column, col_high, col_low, wide, t_high, t_low, tall, result,
    load_sem, a_send, a_recv, shift_sem, sib_send, sib_recv, own_sem, y_send, y_recv,
    z_send, z_recv, x_send, x_recv, f_send, f_recv, c_send, c_recv, d_send, d_recv, out_sem,
):
    r, c = lax.axis_index("row"), lax.axis_index("col")
    hi, y = r // 4, r % 4
    x, z, core = c // 8, (c // 2) % 4, c % 2
    sibling = (r, c + 1 - 2 * core)
    y_next, y_prev = (hi * 4 + (y + 1) % 4, c), (hi * 4 + (y + 3) % 4, c)
    x_next, x_prev = (r, (c + 8) % 32), (r, (c + 24) % 32)
    z_other = [(r, 8 * x + 2 * ((z + d) % 4) + core) for d in (1, 2, 3)]
    c_next, c_prev = (r, (c + 1) % 32), (r, (c + 31) % 32)
    r_next, r_prev = ((r + 1) % 8, c), ((r + 7) % 8, c)
    source_row = c // 4
    to_self = jnp.logical_and(source_row == r, x == y)
    half = at(core * 1024, 1024)
    other_half = at(1024 - core * 1024, 1024)

    loads = [
        pltpu.make_async_copy(h_ref, tile.at[pl.ds(0, ROWS)], load_sem.at[0]),
        pltpu.make_async_copy(z_ref, tile.at[pl.ds(ROWS, ZR)], load_sem.at[1]),
    ]
    u_loads = [
        pltpu.make_async_copy(u_ref.at[k], piece.at[0, :, pl.ds(W * k, W)], load_sem.at[2 + k]) for k in range(4)
    ]
    v_loads = [
        pltpu.make_async_copy(
            v_ref.at[0, :, pl.ds(HALF, HALF)], piece.at[1, :, pl.ds(0, HALF)], load_sem.at[6]
        )
    ] + [
        pltpu.make_async_copy(v_ref.at[k], piece.at[1, :, pl.ds(W * k - HALF, W)], load_sem.at[6 + k])
        for k in range(1, 4)
    ]
    for copy in u_loads + v_loads + loads:
        copy.start()

    barrier = pltpu.get_barrier_semaphore()
    for device in [sibling, y_next, y_prev, x_next, x_prev, c_next, c_prev, r_next, r_prev] + z_other:
        pl.semaphore_signal(barrier, inc=1, device_id=device, device_id_type=MESH)
    for i in range(8):
        source = 8 * y + i

        @pl.when(jnp.logical_not(jnp.logical_and(source_row == r, source == c)))
        def _():
            pl.semaphore_signal(barrier, inc=1, device_id=(source_row, source), device_id_type=MESH)

    pl.semaphore_wait(barrier, 20 - to_self.astype(jnp.int32))

    waits = []

    shift = remote(
        v_ref.at[0, :, pl.ds(0, HALF)], piece.at[1, :, pl.ds(ROWS - HALF, HALF)],
        shift_sem.at[0], shift_sem.at[1], r_prev,
    )
    shift.start()

    def spread_start(t):
        for k in range(4):
            for other in range(2):
                src = piece.at[t, :, pl.ds(W * k, W)]
                dst = column.at[t, at(16 * c, 16), :]
                here = jnp.logical_and(jnp.logical_and(other == hi, x == y), 4 * r + k == c)

                @pl.when(here)
                def _():
                    pltpu.make_async_copy(src, dst, a_recv.at[t]).start()

                @pl.when(jnp.logical_not(here))
                def _():
                    remote(
                        src, dst, a_send.at[t, 2 * k + other], a_recv.at[t], (4 * other + x, 4 * r + k)
                    ).start()

    def spread_sent(t):
        for k in range(4):
            for other in range(2):
                src = piece.at[t, :, pl.ds(W * k, W)]
                dst = column.at[t, at(16 * c, 16), :]
                here = jnp.logical_and(jnp.logical_and(other == hi, x == y), 4 * r + k == c)

                @pl.when(jnp.logical_not(here))
                def _():
                    remote(
                        src, dst, a_send.at[t, 2 * k + other], a_recv.at[t], (4 * other + x, 4 * r + k)
                    ).wait_send()

    def spread_arrived(t):
        group = column.at[t, at(128 * y, 128), :]
        pltpu.make_async_copy(group, group, a_recv.at[t]).wait()

    def ring(t, me, next_device, prev_device, region, part, send, recv):
        def copies(i):
            back, front, far = (i + 3) % 4, (i + 1) % 4, (i + 2) % 4
            out = [
                remote(region(i), region(i), send.at[t, 0], recv.at[t, 0], next_device),
                remote(region(i), region(i), send.at[t, 1], recv.at[t, 1], prev_device),
                remote(part(back, 0), part(back, 0), send.at[t, 2], recv.at[t, 2], next_device),
                remote(part(front, 1), part(front, 1), send.at[t, 3], recv.at[t, 3], prev_device),
            ]
            arrivals = [
                remote(region(back), region(back), send.at[t, 0], recv.at[t, 0], next_device),
                remote(region(front), region(front), send.at[t, 1], recv.at[t, 1], prev_device),
                remote(part(far, 0), part(far, 0), send.at[t, 2], recv.at[t, 2], next_device),
                remote(part(far, 1), part(far, 1), send.at[t, 3], recv.at[t, 3], prev_device),
            ]
            return out, arrivals

        return copies(me)

    y_rings = [
        ring(
            t, y, y_next, y_prev,
            lambda j, t=t: column.at[t, at(128 * j, 128), :],
            lambda j, s, t=t: column.at[t, at(128 * j + 64 * s, 64), :],
            y_send, y_recv,
        )
        for t in range(2)
    ]
    x_rings = [
        ring(
            t, x, x_next, x_prev,
            lambda j, t=t: gathered.at[t, at(128 * j, 128), half],
            lambda j, s, t=t: gathered.at[t, at(128 * j + 64 * s, 64), half],
            x_send, x_recv,
        )
        for t in range(2)
    ]

    def start(copy):
        copy.start()
        waits.append(copy)

    def sibling_start(t):
        start(
            remote(
                piece.at[t, :, other_half], gathered.at[t, at(16 * c, 16), other_half],
                sib_send.at[t], sib_recv.at[t], sibling,
            )
        )
        pltpu.make_async_copy(piece.at[t, :, half], gathered.at[t, at(16 * c, 16), half], own_sem.at[t]).start()

    def sibling_arrived(t):
        rows = at(16 * (c + 1 - 2 * core), 16)
        remote(
            piece.at[t, :, half], gathered.at[t, rows, half], sib_send.at[t], sib_recv.at[t], sibling
        ).wait_recv()
        pltpu.make_async_copy(piece.at[t, :, half], gathered.at[t, at(16 * c, 16), half], own_sem.at[t]).wait()

    def z_start(t):
        ours = gathered.at[t, at(32 * (c // 2), 32), half]
        for i in range(3):
            start(remote(ours, ours, z_send.at[t, i], z_recv.at[t, i], z_other[i]))

    def z_arrived(t):
        for i in range(3):
            theirs = gathered.at[t, at(32 * (4 * x + (z + 3 - i) % 4), 32), half]
            remote(theirs, theirs, z_send.at[t, i], z_recv.at[t, i], z_other[i]).wait_recv()

    def forward(t, j):
        group = gathered.at[t, at(128 * ((x + j) % 4), 128), half]
        start(remote(group, group, f_send.at[t, j], f_recv.at[t, j], sibling))

    def forwarded(t):
        for j in range(4):
            group = gathered.at[t, at(128 * ((x + j) % 4), 128), other_half]
            remote(group, group, f_send.at[t, j], f_recv.at[t, j], sibling).wait_recv()

    def ring_first(ring):
        out, _ = ring
        start(out[0])
        start(out[1])

    def ring_second(ring):
        out, arrivals = ring
        arrivals[0].wait_recv()
        start(out[2])
        arrivals[1].wait_recv()
        start(out[3])

    def ring_last(ring):
        _, arrivals = ring
        arrivals[2].wait_recv()
        arrivals[3].wait_recv()

    def split_column(t):
        high, low = split(column[t])
        col_high[t] = high
        col_low[t] = low

    def strip_copies(b):
        rows = at(256 * b, 256)
        return (
            remote(
                wide.at[rows, pl.ds(256, 256)], wide.at[rows, pl.ds(768, 256)],
                c_send.at[0, b], c_recv.at[0, b], c_prev,
            ),
            remote(
                wide.at[rows, pl.ds(512, 256)], wide.at[rows, pl.ds(0, 256)],
                c_send.at[1, b], c_recv.at[1, b], c_next,
            ),
        )

    def right_first(low, high):
        @pl.loop(low, high)
        def _(position):
            b = block_of(position)
            rows = at(256 * b, 256)
            wide[rows, pl.ds(256, 512)] = plain(split(tile[rows, :]), (col_high[0], col_low[0]))
            for copy in strip_copies(b):
                copy.start()

    def right_second(b, store):
        rows = at(256 * b, 256)
        for copy in strip_copies(b):
            copy.wait_recv()
        for s in range(2):
            cols = pl.ds(256 * s, 256)
            store(
                cols,
                plain(split(wide[rows, pl.ds(512 * s, 512)]), (col_high[1, :, cols], col_low[1, :, cols])),
            )

    row_copies = (
        remote(
            tall.at[pl.ds(256, 256)], tall.at[pl.ds(2304, 256)], d_send.at[0], d_recv.at[0], r_prev
        ),
        remote(
            tall.at[pl.ds(2048, 256)], tall.at[pl.ds(0, 256)], d_send.at[1], d_recv.at[1], r_next
        ),
    )

    def window(position):
        k = window_of(position)

        @pl.loop(0, 2)
        def _(s):
            def store(cols, value):
                high, low = split(value)
                t_high[at(256 * s, 256), cols] = high
                t_low[at(256 * s, 256), cols] = low

            right_second(2 * k + s, store)

        @pl.loop(0, 2)
        def _(s):
            start_row = 512 * k + 256 * s
            tall[at(256 + start_row, 256), :] = turned(
                split(gathered[0, :, at(start_row, 256)]), (t_high[...], t_low[...])
            )

        if position == 0:
            start(row_copies[0])
        if position == 1:
            start(row_copies[1])

    def out_copy(j):
        return pltpu.make_async_copy(
            result.at[at(256 * j, 256)], ho_ref.at[at(256 * j, 256)], out_sem.at[j]
        )

    def left_second(low, high):
        @pl.loop(low, high)
        def _(j):
            result[at(256 * j, 256), :] = turned(
                split(gathered[1, :, at(256 * j, 256)]), split(tall[at(512 * ((j + 1) // 2), 512), :])
            )
            out_copy(j).start()

    for copy in u_loads:
        copy.wait()
    spread_start(0)
    sibling_start(0)
    spread_arrived(0)
    ring_first(y_rings[0])
    sibling_arrived(0)
    z_start(0)
    for copy in v_loads:
        copy.wait()
    shift.wait_recv()
    spread_start(1)
    sibling_start(1)
    ring_second(y_rings[0])
    sibling_arrived(1)
    z_start(1)
    z_arrived(0)
    ring_first(x_rings[0])
    forward(0, 0)
    for copy in loads:
        copy.wait()
    ring_last(y_rings[0])
    split_column(0)
    right_first(0, 4)
    spread_arrived(1)
    ring_first(y_rings[1])
    ring_second(x_rings[0])
    forward(0, 3)
    forward(0, 1)
    right_first(4, 9)
    ring_second(y_rings[1])
    z_arrived(1)
    ring_first(x_rings[1])
    forward(1, 0)
    ring_last(x_rings[0])
    forward(0, 2)
    ring_last(y_rings[1])
    split_column(1)
    forwarded(0)
    window(0)
    ring_second(x_rings[1])
    forward(1, 3)
    forward(1, 1)
    window(1)
    ring_last(x_rings[1])
    forward(1, 2)
    window(2)
    forwarded(1)
    left_second(1, 3)
    window(3)
    left_second(3, 7)

    def store_z(cols, value):
        result[pl.ds(ROWS, ZR), cols] = value

    right_second(8, store_z)
    z_out = pltpu.make_async_copy(result.at[pl.ds(ROWS, ZR)], zo_ref, out_sem.at[8])
    z_out.start()
    row_copies[1].wait_recv()
    left_second(0, 1)
    row_copies[0].wait_recv()
    left_second(7, 8)

    for copy in waits:
        copy.wait_send()
    shift.wait_send()
    spread_sent(0)
    spread_sent(1)

    @pl.loop(0, BLOCKS)
    def _(b):
        for copy in strip_copies(b):
            copy.wait_send()

    @pl.loop(0, 8)
    def _(j):
        out_copy(j).wait()

    z_out.wait()


def per_device(active_matrix, schur_rows, accum_first, accum_second):
    dma = pltpu.SemaphoreType.DMA
    anywhere = pl.BlockSpec(memory_space=pl.ANY)
    return pl.pallas_call(
        kernel,
        out_shape=(
            jax.ShapeDtypeStruct((ROWS, W), F32),
            jax.ShapeDtypeStruct((ZR, W), F32),
        ),
        in_specs=[anywhere] * 4,
        out_specs=[anywhere] * 2,
        scratch_shapes=[
            pltpu.VMEM((ROWS + ZR, W), F32),
            pltpu.VMEM((2, 16, ROWS), F32),
            pltpu.VMEM((2, W, ROWS), F32),
            pltpu.VMEM((2, W, W), F32),
            pltpu.VMEM((2, W, W), BF16),
            pltpu.VMEM((2, W, W), BF16),
            pltpu.VMEM((ROWS + ZR, 2 * W), F32),
            pltpu.VMEM((W, W), BF16),
            pltpu.VMEM((W, W), BF16),
            pltpu.VMEM((ROWS + W, W), F32),
            pltpu.VMEM((ROWS + ZR, W), F32),
            dma((10,)),
            dma((2, 8)),
            dma((2,)),
            dma((2,)),
            dma((2,)),
            dma((2,)),
            dma((2,)),
            dma((2, 4)),
            dma((2, 4)),
            dma((2, 3)),
            dma((2, 3)),
            dma((2, 4)),
            dma((2, 4)),
            dma((2, 4)),
            dma((2, 4)),
            dma((2, BLOCKS)),
            dma((2, BLOCKS)),
            dma((2,)),
            dma((2,)),
            dma((9,)),
        ],
        compiler_params=pltpu.CompilerParams(
            collective_id=0, has_side_effects=True, vmem_limit_bytes=58 * 1024 * 1024
        ),
        cost_estimate=pl.CostEstimate(flops=14_000_000_000, bytes_accessed=20_000_000, transcendentals=0),
    )(active_matrix, schur_rows, accum_first, accum_second)


def solution(mesh):
    in_specs = (P("row", "col"), P("row", "col"), P("row", "col", None), P("row", "col", None))
    out_specs = (P("row", "col"), P("row", "col"))
    return jax.shard_map(
        per_device, mesh=mesh, in_specs=in_specs, out_specs=out_specs, check_vma=False
    )
```

time: 488 us -> 144 us (0.30)
  the two profiles are of different devices: /device:TPU:194 before, /device:TPU:102 now
where the time goes in v1:
time: 144 us
  Pallas kernels  138 us (96%)
  local copies, waits for them, and re-layouts  5.5 us (4%)
    pallas_call x1, Pallas kernels, per_device(): pl.pallas_call(kernel, out_shape=(jax.ShapeDtypeStruct((ROWS, W), F32), j...  138 us
    unnamed x4, local copies, waits for them, and re-layouts  5.5 us

profile of v1, /device:TPU:102, one launch (start us, length us, event | category | flops | bytes accessed | tf_op | source)
XLA Modules:
  0.0 144.1 jit_solution(8037226994377424308)
XLA Ops:
  0.6 137.9 %shard_map.59 = (f32[2048,512]{1,0:T(8,128)}, f32[256,512]{1,0:T(8,128)}) custom-call(f32[2048,512]{1,0:T(8,128)} %h_ref.1, f32[256,512]{1,0:T(8,128)} %z_ref.1, f32[4,16,512]{2,1,0:T(8,128)} %u_ref.1, f32[4,16,512]{2,1,0:T(8,128)} %v_ref.1), custom_call_target="tpu_custom_call" | custom-call | flops 14000000000 | bytes 20000000 | tf_op jit(solution)/shard_map/pallas_call | solution.py:416
  138.6 0.0 copy-start
  138.6 4.7 %copy.8 = f32[2048,512]{1,0:T(8,128)} copy(f32[2048,512]{1,0:T(8,128)} %get-tuple-element.4) | data formatting | bytes 8388608
  143.3 0.0 copy-done
  143.3 0.8 copy.9
Async XLA Ops:
  138.6 4.7 %copy-start = (f32[256,512]{1,0:T(8,128)S(1)}, f32[256,512]{1,0:T(8,128)}, u32[]{:S(2)}) copy-start(f32[256,512]{1,0:T(8,128)} %get-tuple-element.5) | copy-start | bytes 1572868

commit v2 on v1

--- a/solution.py
+++ b/solution.py
@@ -63,7 +63,7 @@
     h_ref, z_ref, u_ref, v_ref, ho_ref, zo_ref,
     tile, piece, gathered, column, col_high, col_low, wide, t_high, t_low, tall, result,
     load_sem, a_send, a_recv, shift_sem, sib_send, sib_recv, own_sem, y_send, y_recv,
-    z_send, z_recv, x_send, x_recv, f_send, f_recv, c_send, c_recv, d_send, d_recv, out_sem,
+    z_send, z_recv, x_send, x_recv, f_send, f_recv, c_send, c_recv, d_send, d_recv, p_sem, detour, out_sem,
 ):
     r, c = lax.axis_index("row"), lax.axis_index("col")
     hi, y = r // 4, r % 4
@@ -76,6 +76,10 @@
     r_next, r_prev = ((r + 1) % 8, c), ((r + 7) % 8, c)
     source_row = c // 4
     to_self = jnp.logical_and(source_row == r, x == y)
+    relays = jnp.logical_or(y == 1, y == 2)
+    relay_to = (hi * 4 + jnp.where(y == 0, 1, 2), c)
+    relay_on = ((1 - hi) * 4 + jnp.where(y == 1, 3, 0), c)
+    relay_by = ((1 - hi) * 4 + jnp.where(y == 3, 1, 2), c)
     half = at(core * 1024, 1024)
     other_half = at(1024 - core * 1024, 1024)
 
@@ -98,16 +102,28 @@
         copy.start()
 
     barrier = pltpu.get_barrier_semaphore()
+    def hello(device):
+        pl.semaphore_signal(barrier, inc=1, device_id=device, device_id_type=MESH)
+
     for device in [sibling, y_next, y_prev, x_next, x_prev, c_next, c_prev, r_next, r_prev] + z_other:
-        pl.semaphore_signal(barrier, inc=1, device_id=device, device_id_type=MESH)
+        hello(device)
+
+    @pl.when(jnp.logical_not(relays))
+    def _():
+        hello(relay_by)
+
     for i in range(8):
         source = 8 * y + i
 
         @pl.when(jnp.logical_not(jnp.logical_and(source_row == r, source == c)))
         def _():
-            pl.semaphore_signal(barrier, inc=1, device_id=(source_row, source), device_id_type=MESH)
-
-    pl.semaphore_wait(barrier, 20 - to_self.astype(jnp.int32))
+            hello((source_row, source))
+
+    number = jnp.int32
+    pl.semaphore_wait(
+        barrier,
+        20 + relays.astype(number) - to_self.astype(number),
+    )
 
     waits = []
 
@@ -283,14 +299,52 @@
                 plain(split(wide[rows, pl.ds(512 * s, 512)]), (col_high[1, :, cols], col_low[1, :, cols])),
             )
 
-    row_copies = (
-        remote(
-            tall.at[pl.ds(256, 256)], tall.at[pl.ds(2304, 256)], d_send.at[0], d_recv.at[0], r_prev
-        ),
-        remote(
-            tall.at[pl.ds(2048, 256)], tall.at[pl.ds(0, 256)], d_send.at[1], d_recv.at[1], r_next
-        ),
-    )
+    def row_strip(way, part):
+        src = tall.at[pl.ds((256, 2048)[way] + 128 * part, 128)]
+        dst = tall.at[pl.ds((2304, 0)[way] + 128 * part, 128)]
+        return remote(src, dst, d_send.at[way, part], d_recv.at[way, part], (r_prev, r_next)[way])
+
+    def row_detour(way):
+        src = tall.at[pl.ds((256, 2048)[way] + 128, 128)]
+        return remote(src, detour, d_send.at[way, 1], p_sem.at[0], relay_to)
+
+    def row_start(way):
+        crosses = y == (0, 3)[way]
+        start(row_strip(way, 0))
+
+        @pl.when(crosses)
+        def _():
+            row_detour(way).start()
+
+        @pl.when(jnp.logical_not(crosses))
+        def _():
+            row_strip(way, 1).start()
+
+    def row_sent(way):
+        row_strip(way, 1).wait_send()
+
+    def row_arrived(way):
+        for part in range(2):
+            row_strip(way, part).wait_recv()
+
+    def relay(way):
+        dst = tall.at[pl.ds((2304, 0)[way] + 128, 128)]
+        return remote(detour, dst, p_sem.at[1], d_recv.at[way, 1], relay_on)
+
+    def relay_start():
+        for way in range(2):
+
+            @pl.when(y == (1, 2)[way])
+            def _():
+                remote(detour, detour, p_sem.at[1], p_sem.at[0], relay_to).wait_recv()
+                relay(way).start()
+
+    def relay_sent():
+        for way in range(2):
+
+            @pl.when(y == (1, 2)[way])
+            def _():
+                relay(way).wait_send()
 
     def window(position):
         k = window_of(position)
@@ -311,10 +365,8 @@
                 split(gathered[0, :, at(start_row, 256)]), (t_high[...], t_low[...])
             )
 
-        if position == 0:
-            start(row_copies[0])
-        if position == 1:
-            start(row_copies[1])
+        if position < 2:
+            row_start(position)
 
     def out_copy(j):
         return pltpu.make_async_copy(
@@ -333,36 +385,36 @@
         copy.wait()
     spread_start(0)
     sibling_start(0)
-    spread_arrived(0)
-    ring_first(y_rings[0])
     sibling_arrived(0)
     z_start(0)
     for copy in v_loads:
         copy.wait()
     shift.wait_recv()
-    spread_start(1)
     sibling_start(1)
-    ring_second(y_rings[0])
+    spread_arrived(0)
+    ring_first(y_rings[0])
     sibling_arrived(1)
     z_start(1)
-    z_arrived(0)
-    ring_first(x_rings[0])
-    forward(0, 0)
+    ring_second(y_rings[0])
     for copy in loads:
         copy.wait()
     ring_last(y_rings[0])
     split_column(0)
+    spread_start(1)
     right_first(0, 4)
+    z_arrived(0)
+    ring_first(x_rings[0])
+    forward(0, 0)
+    right_first(4, 9)
     spread_arrived(1)
     ring_first(y_rings[1])
     ring_second(x_rings[0])
     forward(0, 3)
     forward(0, 1)
-    right_first(4, 9)
-    ring_second(y_rings[1])
     z_arrived(1)
     ring_first(x_rings[1])
     forward(1, 0)
+    ring_second(y_rings[1])
     ring_last(x_rings[0])
     forward(0, 2)
     ring_last(y_rings[1])
@@ -376,6 +428,7 @@
     ring_last(x_rings[1])
     forward(1, 2)
     window(2)
+    relay_start()
     forwarded(1)
     left_second(1, 3)
     window(3)
@@ -387,16 +440,18 @@
     right_second(8, store_z)
     z_out = pltpu.make_async_copy(result.at[pl.ds(ROWS, ZR)], zo_ref, out_sem.at[8])
     z_out.start()
-    row_copies[1].wait_recv()
+    row_arrived(1)
     left_second(0, 1)
-    row_copies[0].wait_recv()
+    row_arrived(0)
     left_second(7, 8)
 
     for copy in waits:
         copy.wait_send()
     shift.wait_send()
-    spread_sent(0)
-    spread_sent(1)
+    for t in range(2):
+        spread_sent(t)
+        row_sent(t)
+    relay_sent()
 
     @pl.loop(0, BLOCKS)
     def _(b):
@@ -443,15 +498,17 @@
             dma((2, 4)),
             dma((2, 4)),
             dma((2, 3)),
-            dma((2, 3)),
+            dma((2, 4)),
             dma((2, 4)),
             dma((2, 4)),
             dma((2, 4)),
             dma((2, 4)),
             dma((2, BLOCKS)),
             dma((2, BLOCKS)),
+            dma((2, 2)),
+            dma((2, 2)),
             dma((2,)),
-            dma((2,)),
+            pltpu.VMEM((128, W), F32),
             dma((9,)),
         ],
         compiler_params=pltpu.CompilerParams(

time: 144 us -> 133 us (0.924)
  Pallas kernels: 138 us -> 126 us
    pallas_call x1, Pallas kernels: 138 us -> 126 us  [per_device(): pl.pallas_call(kernel, out_shape=(jax.ShapeDtypeStruct((ROWS, W), F32), j...]
where the time goes in v2:
time: 133 us; the launch traced here: 132 us
  Pallas kernels  126 us (95%)
  local copies, waits for them, and re-layouts  5.5 us (4%)
    pallas_call x1, Pallas kernels, per_device(): pl.pallas_call(kernel, out_shape=(jax.ShapeDtypeStruct((ROWS, W), F32), j...  126 us
    unnamed x4, local copies, waits for them, and re-layouts  5.5 us

profile of v2, /device:TPU:102, one launch (start us, length us, event | category | flops | bytes accessed | tf_op | source)
XLA Modules:
  0.0 132.0 jit_solution(5712902983049550266)
XLA Ops:
  0.6 125.9 %shard_map.59 = (f32[2048,512]{1,0:T(8,128)}, f32[256,512]{1,0:T(8,128)}) custom-call(f32[2048,512]{1,0:T(8,128)} %h_ref.1, f32[256,512]{1,0:T(8,128)} %z_ref.1, f32[4,16,512]{2,1,0:T(8,128)} %u_ref.1, f32[4,16,512]{2,1,0:T(8,128)} %v_ref.1), custom_call_target="tpu_custom_call" | custom-call | flops 14000000000 | bytes 20000000 | tf_op jit(solution)/shard_map/pallas_call | solution.py:471
  126.5 0.0 copy-start
  126.5 4.7 %copy.8 = f32[2048,512]{1,0:T(8,128)} copy(f32[2048,512]{1,0:T(8,128)} %get-tuple-element.4) | data formatting | bytes 8388608
  131.2 0.0 copy-done
  131.2 0.8 copy.9
Async XLA Ops:
  126.5 4.7 %copy-start = (f32[256,512]{1,0:T(8,128)S(1)}, f32[256,512]{1,0:T(8,128)}, u32[]{:S(2)}) copy-start(f32[256,512]{1,0:T(8,128)} %get-tuple-element.5) | copy-start | bytes 1572868

commit v3 on v2

--- a/solution.py
+++ b/solution.py
@@ -167,14 +167,19 @@
         group = column.at[t, at(128 * y, 128), :]
         pltpu.make_async_copy(group, group, a_recv.at[t]).wait()
 
-    def ring(t, me, next_device, prev_device, region, part, send, recv):
+    def ring(t, me, next_device, prev_device, region, part, send, recv, all_prev, all_next):
         def copies(i):
             back, front, far = (i + 3) % 4, (i + 1) % 4, (i + 2) % 4
+            def pick(condition, yes, no):
+                return tuple(jnp.where(condition, a, b) for a, b in zip(yes, no))
+
+            first = part(jnp.where(all_prev, front, back), 0)
+            second = part(jnp.where(all_next, back, front), 1)
             out = [
                 remote(region(i), region(i), send.at[t, 0], recv.at[t, 0], next_device),
                 remote(region(i), region(i), send.at[t, 1], recv.at[t, 1], prev_device),
-                remote(part(back, 0), part(back, 0), send.at[t, 2], recv.at[t, 2], next_device),
-                remote(part(front, 1), part(front, 1), send.at[t, 3], recv.at[t, 3], prev_device),
+                remote(first, first, send.at[t, 2], recv.at[t, 2], pick(all_prev, prev_device, next_device)),
+                remote(second, second, send.at[t, 3], recv.at[t, 3], pick(all_next, next_device, prev_device)),
             ]
             arrivals = [
                 remote(region(back), region(back), send.at[t, 0], recv.at[t, 0], next_device),
@@ -191,7 +196,7 @@
             t, y, y_next, y_prev,
             lambda j, t=t: column.at[t, at(128 * j, 128), :],
             lambda j, s, t=t: column.at[t, at(128 * j + 64 * s, 64), :],
-            y_send, y_recv,
+            y_send, y_recv, False, False,
         )
         for t in range(2)
     ]
@@ -200,7 +205,7 @@
             t, x, x_next, x_prev,
             lambda j, t=t: gathered.at[t, at(128 * j, 128), half],
             lambda j, s, t=t: gathered.at[t, at(128 * j + 64 * s, 64), half],
-            x_send, x_recv,
+            x_send, x_recv, jnp.logical_and(t == 1, z == 0), jnp.logical_and(t == 1, z == 3),
         )
         for t in range(2)
     ]
@@ -249,11 +254,14 @@
         start(out[0])
         start(out[1])
 
-    def ring_second(ring):
+    def ring_second(ring, one_way=False):
         out, arrivals = ring
         arrivals[0].wait_recv()
+        if one_way:
+            arrivals[1].wait_recv()
         start(out[2])
-        arrivals[1].wait_recv()
+        if not one_way:
+            arrivals[1].wait_recv()
         start(out[3])
 
     def ring_last(ring):
@@ -421,7 +429,7 @@
     split_column(1)
     forwarded(0)
     window(0)
-    ring_second(x_rings[1])
+    ring_second(x_rings[1], one_way=True)
     forward(1, 3)
     forward(1, 1)
     window(1)

time: 133 us -> 136 us (1.023)
  Pallas kernels: 126 us -> 129 us
    pallas_call x1, Pallas kernels: 126 us -> 129 us  [per_device(): pl.pallas_call(kernel, out_shape=(jax.ShapeDtypeStruct((ROWS, W), F32), j...]
where the time goes in v3:
time: 136 us
  Pallas kernels  129 us (95%)
  local copies, waits for them, and re-layouts  5.5 us (4%)
    pallas_call x1, Pallas kernels, per_device(): pl.pallas_call(kernel, out_shape=(jax.ShapeDtypeStruct((ROWS, W), F32), j...  129 us
    unnamed x4, local copies, waits for them, and re-layouts  5.5 us

profile of v3, /device:TPU:102, one launch (start us, length us, event | category | flops | bytes accessed | tf_op | source)
XLA Modules:
  0.0 135.6 jit_solution(10722848199861833421)
XLA Ops:
  0.6 129.5 %shard_map.59 = (f32[2048,512]{1,0:T(8,128)}, f32[256,512]{1,0:T(8,128)}) custom-call(f32[2048,512]{1,0:T(8,128)} %h_ref.1, f32[256,512]{1,0:T(8,128)} %z_ref.1, f32[4,16,512]{2,1,0:T(8,128)} %u_ref.1, f32[4,16,512]{2,1,0:T(8,128)} %v_ref.1), custom_call_target="tpu_custom_call" | custom-call | flops 14000000000 | bytes 20000000 | tf_op jit(solution)/shard_map/pallas_call | solution.py:479
  130.1 0.0 copy-start
  130.1 4.7 %copy.8 = f32[2048,512]{1,0:T(8,128)} copy(f32[2048,512]{1,0:T(8,128)} %get-tuple-element.4) | data formatting | bytes 8388608
  134.8 0.0 copy-done
  134.8 0.8 copy.9
Async XLA Ops:
  130.1 4.7 %copy-start = (f32[256,512]{1,0:T(8,128)S(1)}, f32[256,512]{1,0:T(8,128)}, u32[]{:S(2)}) copy-start(f32[256,512]{1,0:T(8,128)} %get-tuple-element.5) | copy-start | bytes 1572868
